TPU v7x, 32 devices: a whole 2x2x4 slice. The times are simulated.
32 devices in a mesh: parts: 2 (over y), tensor: 4 (over z), group: 2 (over x), rep: 2 (over core).
Axes of the slice: x: 2, y: 2, z: 4, core: 2. Of those that a mesh axis runs over, the one named last changes fastest.
Arguments:
- hidden_rows: bfloat16 [512, 28672], P(('parts', 'tensor'), ('group', 'rep')), parts along dimension 0, may hold values from -6 to 6
- down_weight: bfloat16 [28672, 8192], P(('group', 'rep'), 'tensor'), may hold values from -0.03125 to 0.03125
- adapter_down: bfloat16 [8, 28672, 64], P('tensor', ('group', 'rep')), may hold values from -0.03125 to 0.03125
- adapter_up: bfloat16 [8, 64, 8192], P(('group', 'rep'), None, 'tensor'), may hold values from -0.75 to 0.75
- adapter_id: int32 [512, 1], P('parts'), parts along dimension 0, may hold values from 0 to 7; in each aligned block of 256 rows (0 to 255, 256 to 511, ...) at most 128 rows name the same one
- adapter_slot: int32 [8], replicated, may hold values from 0 to 7, each once
Outputs:
- scored: bfloat16 [512, 8192], P(('parts', 'group', 'rep'), 'tensor'), parts along dimension 0
There are 2 independent parts, one for each index of `parts`. A program takes and returns all parts, laid end to end along the dimension named above; an argument that names none is the same for every part. Nothing has to cross between parts.
Inputs may be any that keep to these rules, and one draw needn't show every extreme that they name: `adapter_id`: at most 128 rows of one part name the same adapter, every row names one adapter, and every adapter is named by some row. A permutation: adapter a's factors lie at index adapter_slot[a] of adapter_down and adapter_up.
All inputs are finite; a program needn't handle non-finite values.
Results may differ from a plain program's by a relative error of at most 0.0032.
Values may be sent and summed in bfloat16 or wider, within the bound.
A program may use at most 128 MiB of HBM per device.

v0:
```python
import jax
import jax.numpy as jnp
from jax import lax
from jax.sharding import PartitionSpec as P

adapter_scale = 0.5


def on_device(hidden_rows, down_weight, adapter_down, adapter_up, adapter_id, adapter_slot):
    total_rows = adapter_id.shape[0]
    adapters = adapter_slot.shape[0]
    local_slots = adapter_down.shape[0]
    rank_width = adapter_down.shape[2]
    group_width = lax.axis_size(("group", "rep"))
    out_rows = total_rows // group_width
    capacity = 2 * (total_rows // lax.axis_size("tensor"))
    row_ids = adapter_id[:, 0]
    slot_table = jnp.arange(adapters, dtype=jnp.int32)
    matches = row_ids[:, None] == slot_table[None, :]
    slot_of_row = jnp.sum(jnp.where(matches, adapter_slot[None, :], 0), axis=1)
    member = slot_of_row[:, None] == slot_table[None, :]
    counts = jnp.sum(member.astype(jnp.int32), axis=0)
    offsets = jnp.cumsum(counts) - counts
    sort_order = jnp.argsort(slot_of_row, stable=True)
    positions = jnp.arange(total_rows, dtype=jnp.int32)
    sorted_position_index = jnp.zeros((total_rows,), jnp.int32).at[sort_order].set(positions)
    within = sorted_position_index - jnp.sum(jnp.where(member, offsets[None, :], 0), axis=1)
    gathered = lax.all_gather(hidden_rows, "tensor", axis=0, tiled=True)
    first_slot = lax.axis_index("tensor") * local_slots
    my_slots = first_slot + jnp.arange(local_slots, dtype=jnp.int32)
    lane_index = jnp.arange(capacity, dtype=jnp.int32)
    seg_begin = offsets[my_slots]
    pick_index = jnp.clip(seg_begin[:, None] + lane_index[None, :], 0, total_rows - 1)
    rows_index = sort_order[pick_index]
    is_valid = lane_index[None, :] < counts[my_slots][:, None]
    picked = jnp.where(is_valid[:, :, None], gathered[rows_index], jnp.zeros((), jnp.bfloat16))
    partial_rank = jnp.einsum(
        "scf,sfk->sck", picked, adapter_down, preferred_element_type=jnp.float32
    )
    summed = lax.psum(partial_rank, ("group", "rep"))
    every_low_rank_output = lax.all_gather(
        summed.astype(jnp.bfloat16), "tensor", axis=0, tiled=True
    )
    flat_rows = every_low_rank_output.reshape(adapters * capacity, rank_width)
    every_lowrank = flat_rows[slot_of_row * capacity + within]
    own_index = lax.axis_index(("group", "rep"))
    plain_row_outputs = lax.psum_scatter(
        jnp.dot(gathered, down_weight, preferred_element_type=jnp.float32),
        ("group", "rep"),
        scatter_dimension=0,
        tiled=True,
    )
    block_start = own_index * out_rows
    row_slots = lax.dynamic_slice_in_dim(slot_of_row, block_start, out_rows, 0)
    lowrank_rows = lax.dynamic_slice_in_dim(every_lowrank, block_start, out_rows, 0)
    factors = lax.all_gather(adapter_up, ("group", "rep"), axis=0, tiled=True)
    chosen = (row_slots[:, None] == slot_table[None, :])[:, :, None]
    spread = jnp.where(chosen, lowrank_rows[:, None, :], jnp.zeros((), jnp.bfloat16))
    spread = spread.reshape(out_rows, adapters * rank_width)
    adapter_row_outputs = jnp.dot(
        spread, factors.reshape(adapters * rank_width, -1), preferred_element_type=jnp.float32
    )
    projected_output = plain_row_outputs + adapter_scale * adapter_row_outputs
    return projected_output.astype(jnp.bfloat16)


def solution(mesh):
    placed = (
        P(("parts", "tensor"), ("group", "rep")),
        P(("group", "rep"), "tensor"),
        P("tensor", ("group", "rep"), None),
        P(("group", "rep"), None, "tensor"),
        P("parts", None),
        P(),
    )
    return jax.shard_map(
        on_device,
        mesh=mesh,
        in_specs=placed,
        out_specs=P(("parts", "group", "rep"), "tensor"),
        check_vma=False,
    )
```

profile of v0, /device:TPU:0, one launch (start us, length us, event | category | flops | bytes accessed | tf_op | source)
XLA Modules:
  0.0 160.2 jit_solution(2294421056866238461)
XLA Ops:
  6.5 0.0 copy-start
  6.5 0.0 all-gather.3.cloned.1.call-start
  6.5 0.7 all-gather.3.cloned.1.call-update
  7.3 0.0 all-gather.5.cloned.1.call-start
  7.3 0.7 all-gather.5.cloned.1.call-update
  8.0 0.0 copy-start.1
  8.0 0.0 copy-start.2
  8.0 0.0 reduce-scatter.2.cloned.1.call-start
  8.1 75.7 %all-gather.3.cloned.1.call-done = bf16[256,7168]{1,0:T(8,128)(2,1)} async-done(((bf16[64,7168]{1,0:T(8,128)(2,1)}), bf16[256,7168]{1,0:T(8,128)(2,1)}) %all-gather.3.cloned.1.call-update) | async-done | bytes 3670032 | tf_op jit(solution)/shard_map/all_gather | solution.py:28
  83.8 16.0 %fusion.18 = f32[256,2048]{1,0:T(8,128)} fusion(bf16[256,7168]{1,0:T(8,128)(2,1)} %all-gather.3.cloned.1.call-done, bf16[7168,2048]{1,0:T(8,128)(2,1)} %param.7), kind=kOutput, calls=%fused_computation.43 | convolution fusion | flops 7516192768 | bytes 35127296 | tf_op jit(solution)/shard_map/dot_general | solution.py:48
  99.8 0.0 reduce-scatter.2.cloned.1.call-update
  99.9 0.0 copy-done.1
  99.9 0.0 copy-done.2
  99.9 0.1 select_reduce_fusion.1
  100.0 0.1 convert_reduce_fusion
  100.1 0.6 gather_fusion
  100.7 0.2 reduce-window.7
  100.9 0.6 gather_fusion.1
  101.6 3.2 %sort.17 = (s32[256]{0:T(256)}, s32[256]{0:T(256)S(1)}) sort(s32[256]{0:T(256)S(1)} %select_reduce_fusion.1, s32[256]{0:T(256)S(1)} %iota.30), dimensions={0}, to_apply=%region_3.4 | sort | flops 2048 | bytes 4096 | tf_op jit(solution)/shard_map/jit(argsort)/sort | solution.py:24
  104.7 0.1 dynamic_slice.6
  104.8 0.1 fusion.11
  104.9 1.9 %gather_fusion.2 = s32[256]{0:T(256)S(1)} fusion(s32[256]{0:T(256)S(1)} %get-tuple-element.6, s32[1024]{0:T(1024)S(1)} %pad_clamp_fusion.2), kind=kCustom, calls=%fused_computation.2 | custom fusion | bytes 3072 | tf_op jit(solution)/shard_map/gather | solution.py:34
  106.9 1.6 scatter_custom_fusion
  108.5 0.1 select_reduce_fusion
  108.6 0.1 iota_compare_fusion.3
  108.7 10.5 %gather_fusion.3 = bf16[256,7168]{1,0:T(8,128)(2,1)} fusion(bf16[256,7168]{1,0:T(8,128)(2,1)} %all-gather.3.cloned.1.call-done, s32[1024]{0:T(1024)S(1)} %pad_clamp_fusion.1), kind=kCustom, calls=%fused_computation.3 | custom fusion | bytes 7341056 | tf_op jit(solution)/shard_map/gather | solution.py:36
  119.2 0.0 copy-done
  119.2 3.5 %fusion = f32[2,128,64]{1,2,0:T(8,128)S(1)} fusion(bf16[2,7168,64]{1,2,0:T(8,128)(2,1)S(1)} %copy-done, bf16[2,128,7168]{2,1,0:T(8,128)(2,1)} %bitcast.27, pred[2,128]{1,0:T(4,128)(4,1)S(1)} %iota_compare_fusion.3), kind=kOutput, calls=%fused_computation.6 | convolution fusion | flops 236716032 | bytes 5570816 | tf_op jit(solution)/shard_map/scf,sfk->sck/dot_general | solution.py:37
  122.7 13.5 %psum.7 = bf16[2,128,64]{1,2,0:T(8,128)(2,1)S(1)} all-reduce(f32[2,128,64]{1,2,0:T(8,128)S(1)} %fusion), channel_id=1, replica_groups=mesh['parts'=2,'tensor'=4,'group'=2,'rep'=2] {'group','rep'}, use_global_device_ids=true, to_apply=%region_5.6 | all-reduce | flops 16384 | bytes 98304 | tf_op jit(solution)/shard_map/psum | solution.py:40
  136.2 13.4 %all_gather.10 = bf16[8,128,64]{1,2,0:T(8,128)(2,1)S(1)} all-gather(bf16[2,128,64]{1,2,0:T(8,128)(2,1)S(1)} %psum.7), channel_id=1, replica_groups=mesh['parts'=2,'tensor'=4,'group'=2,'rep'=2] {'tensor'}, dimensions={0}, use_global_device_ids=true | all-gather | bytes 163840 | tf_op jit(solution)/shard_map/all_gather | solution.py:41
  149.6 0.2 copy.13
  149.8 0.9 gather_fusion.4
  150.7 0.0 all-gather.5.cloned.1.call-done
  150.7 0.0 reduce-scatter.2.cloned.1.call-done
  150.7 3.0 %fusion.5 = bf16[64,2048]{1,0:T(8,128)(2,1)} fusion(f32[64,2048]{1,0:T(8,128)} %reduce-scatter.2.cloned.1.call-done, bf16[8,64,2048]{2,1,0:T(8,128)(2,1)} %all-gather.5.cloned.1.call-done, pred[64,8]{0,1:T(8,128)(4,1)S(1)} %iota_compare_fusion.2, bf16[64,64]{1,0:T(8,128)(2,1)S(1)} %constant_dynamic-slice_fusion), kind=kOutput, calls=%fused_computation.12 | convolution fusion | flops 134643712 | bytes 2892288 | tf_op jit(solution)/shard_map/dot_general | solution.py:60
  (13 shorter events, 0.1 us)
Async XLA Ops:
  6.5 112.7 %copy-start = (bf16[2,7168,64]{1,2,0:T(8,128)(2,1)S(1)}, bf16[2,7168,64]{1,2,0:T(8,128)(2,1)}, u32[]{:S(2)}) copy-start(bf16[2,7168,64]{1,2,0:T(8,128)(2,1)} %param.8) | copy-start | bytes 5505028
  6.5 77.2 %all-gather.3.cloned.1.call-start = ((), (), s32[]{:S(2)}) async-start(), calls=%async_computation.1 | async-start | bytes 4587520 | tf_op jit(solution)/shard_map/all_gather | solution.py:28
  7.3 143.4 %all-gather.5.cloned.1.call-start = ((), (), s32[]{:S(2)}) async-start(), calls=%async_computation.3 | async-start | bytes 2621440 | tf_op jit(solution)/shard_map/all_gather | solution.py:56
  8.0 91.9 %copy-start.1 = (s32[256,1]{0,1:T(1,128)S(1)}, s32[256,1]{0,1:T(1,128)}, u32[]{:S(2)}) copy-start(s32[256,1]{0,1:T(1,128)} %param.10) | copy-start | bytes 3076
  8.0 91.9 %copy-start.2 = (s32[8]{0:T(128)S(1)}, s32[8]{0:T(128)}, u32[]{:S(2)}) copy-start(s32[8]{0:T(128)} %param.11) | copy-start | bytes 100
  8.0 142.7 %reduce-scatter.2.cloned.1.call-start = ((), (), s32[]{:S(2)}) async-start(), calls=%async_computation.2 | async-start | bytes 2621440 | tf_op jit(solution)/shard_map/reduce_scatter | solution.py:47
Sparse Core Ops, SparseCore 0:
  8.9 74.7 all-gather.2
  85.3 21.1 all-gather.4
  109.1 32.1 reduce-scatter.1
where the time goes:
time: 160 us
  waiting for transfers between devices  77.2 us (48%)
  blocking collectives  26.9 us (17%)
  matrix products  22.5 us (14%)
  local copies, waits for them, and re-layouts  16.5 us (10%)
  between operations  13.3 us (8%)
  other arithmetic  3.85 us (2%)
    all_gather x1, waiting for transfers between devices, on_device(): gathered = lax.all_gather(hidden_rows, 'tensor', axis=0, tiled=True)  75.7 us
    dot_general x1, matrix products, on_device(): jnp.dot(gathered, down_weight, preferred_element_type=jnp.float32)  16 us
    psum x1, blocking collectives, on_device(): summed = lax.psum(partial_rank, ('group', 'rep'))  13.5 us
    all_gather x1, blocking collectives, on_device(): lax.all_gather(summed.astype(jnp.bfloat16), 'tensor', axis=0, tiled=True)  13.4 us
    gather x1, local copies, waits for them, and re-layouts, on_device(): gathered[rows_index]  10.5 us
    dot_general x1, matrix products, on_device(): jnp.einsum('scf,sfk->sck', picked, adapter_down, preferred_element_type=j...  3.47 us
  transfers between devices with their start and end apart: 3, of which 1 were waited for; matrix products, arithmetic and copies ran while one was open for 25% of the time, Pallas kernels for 0%

commit v1 on v0

v1 whole, which is shorter than its diff:
```python
import functools
import jax
import jax.numpy as jnp
from jax import lax
from jax.experimental import pallas as pl
from jax.experimental.pallas import tpu as pltpu
from jax.sharding import PartitionSpec as P

adapter_scale = 0.5
MESH = pl.DeviceIdType.MESH


def kernel(
    nt, ng, nr, nk, tile,
    h_ref, w_ref, a_ref, up_ref, id_ref, slot_ref, out_ref,
    wv, av, hbuf, upbuf, acc, racc, rsend, halfbuf, basebuf, rankbuf, lrbuf,
    w_sem, a_sem, own_sem, up_own_sem, flow_send, flow_recv, up_send, up_recv,
    half_send, half_recv, base_send, base_recv, rank_send, rank_recv, lr_send, lr_recv,
):
    t, g, r = lax.axis_index("tensor"), lax.axis_index("group"), lax.axis_index("rep")
    nq = ng * nr
    q = g * nr + r
    per_owner = nt // nq
    rows, depth = h_ref.shape
    width = w_ref.shape[1]
    half = width // nr
    kc = depth // nk
    slots, _, rank = av.shape
    lanes = slots * rank
    up_rows = up_ref.shape[0]
    adapters = slot_ref.shape[0]

    def cols(c):
        return pl.ds(pl.multiple_of(c * kc, 128), kc)

    def half_cols(index):
        return pl.ds(pl.multiple_of(index * half, 128), half)

    def lane_cols(index):
        return pl.ds(pl.multiple_of(index * lanes, 128), lanes)

    def flow(direction, block, c, own):
        source = h_ref.at[:, cols(c)] if own else hbuf.at[block, :, cols(c)]
        target = t + 1 if direction == 0 else t - 1
        return pltpu.make_async_remote_copy(
            src_ref=source, dst_ref=hbuf.at[block, :, cols(c)],
            send_sem=flow_send.at[direction, block, c], recv_sem=flow_recv.at[block, c],
            device_id={"tensor": target}, device_id_type=MESH)

    def w_copy(c):
        part = pl.ds(pl.multiple_of(c * kc, 128), kc)
        return pltpu.make_async_copy(w_ref.at[part], wv.at[part], w_sem.at[c])

    def up_rows_of(index):
        return pl.ds(pl.multiple_of(index * up_rows, 16), up_rows)

    def up_copy(index, source):
        return pltpu.make_async_remote_copy(
            src_ref=up_ref, dst_ref=upbuf.at[up_rows_of(source)],
            send_sem=up_send.at[index], recv_sem=up_recv.at[source],
            device_id={"group": index // nr, "rep": index % nr}, device_id_type=MESH)

    def half_copy(block):
        return pltpu.make_async_remote_copy(
            src_ref=acc.at[block, :, half_cols(1 - r)], dst_ref=halfbuf.at[block],
            send_sem=half_send.at[block], recv_sem=half_recv.at[block],
            device_id={"rep": 1 - r}, device_id_type=MESH)

    def base_copy(block, owner, place):
        return pltpu.make_async_remote_copy(
            src_ref=acc.at[block, :, half_cols(r)], dst_ref=basebuf.at[place, g, r],
            send_sem=base_send.at[block], recv_sem=base_recv.at[place, g * nr + r],
            device_id={"group": owner // nr, "rep": owner % nr}, device_id_type=MESH)

    def rank_copy(block, owner, place):
        return pltpu.make_async_remote_copy(
            src_ref=rsend.at[block], dst_ref=rankbuf.at[place, q],
            send_sem=rank_send.at[block], recv_sem=rank_recv.at[place, q],
            device_id={"group": owner // nr, "rep": owner % nr}, device_id_type=MESH)

    def lr_copy(place, target, source):
        return pltpu.make_async_remote_copy(
            src_ref=lrbuf.at[place, :, lane_cols(source)],
            dst_ref=lrbuf.at[place, :, lane_cols(source)],
            send_sem=lr_send.at[place, target], recv_sem=lr_recv.at[place, source],
            device_id={"tensor": target}, device_id_type=MESH)

    own_copy = pltpu.make_async_copy(h_ref, hbuf.at[t], own_sem)
    a_copy = pltpu.make_async_copy(a_ref, av, a_sem)
    up_own = pltpu.make_async_copy(up_ref, upbuf.at[up_rows_of(q)], up_own_sem)

    own_copy.start()
    a_copy.start()

    @pl.loop(0, nk)
    def _(c):
        w_copy(c).start()

    up_own.start()

    barrier = pltpu.get_barrier_semaphore()

    @pl.loop(0, nt)
    def _(other):
        @pl.when(other != t)
        def _():
            pl.semaphore_signal(barrier, inc=1, device_id={"tensor": other}, device_id_type=MESH)

    @pl.loop(0, nq)
    def _(other):
        @pl.when(other != q)
        def _():
            pl.semaphore_signal(
                barrier, inc=1, device_id={"group": other // nr, "rep": other % nr},
                device_id_type=MESH)

    pl.semaphore_wait(barrier, nt + nq - 2)

    @pl.loop(0, nk)
    def _(c):
        @pl.when(t + 1 < nt)
        def _():
            flow(0, t, c, True).start()

        @pl.when(t > 0)
        def _():
            flow(1, t, c, True).start()

    @pl.loop(0, nq)
    def _(other):
        @pl.when(other != q)
        def _():
            up_copy(other, q).start()

    acc[...] = jnp.zeros_like(acc)
    racc[...] = jnp.zeros_like(racc)

    def multiply(block, c):
        x = hbuf[block, :, cols(c)]

        @pl.loop(0, width // tile)
        def _(n):
            at = pl.ds(pl.multiple_of(n * tile, 128), tile)
            acc[block, :, at] += jnp.dot(
                x, wv[cols(c), at], preferred_element_type=jnp.float32)

        racc[block] += jnp.concatenate(
            [jnp.dot(x, av[s, cols(c), :], preferred_element_type=jnp.float32)
             for s in range(slots)], axis=1)

    def finish(block):
        owner, place = block // per_owner, block % per_owner
        ids = id_ref[pl.ds(pl.multiple_of(block * rows, rows), rows), :]
        row_slot = jnp.zeros_like(ids)
        for adapter in range(adapters):
            row_slot = row_slot + jnp.where(ids == adapter, slot_ref[adapter], 0)
        lane = lax.broadcasted_iota(jnp.int32, (rows, lanes), 1)
        first = (row_slot - t * slots) * rank
        masked = jnp.where((lane >= first) & (lane < first + rank), racc[block], 0.0)

        @pl.when(owner == q)
        def _():
            rankbuf[place, q] = masked

        @pl.when(owner != q)
        def _():
            rsend[block] = masked
            rank_copy(block, owner, place).start()

        half_copy(block).start()

    def combine(block):
        owner, place = block // per_owner, block % per_owner
        half_copy(block).wait_recv()
        value = acc[block, :, half_cols(r)] + halfbuf[block]

        @pl.when(owner == q)
        def _():
            basebuf[place, g, r] = value

        @pl.when(owner != q)
        def _():
            acc[block, :, half_cols(r)] = value
            base_copy(block, owner, place).start()

    own_copy.wait()
    a_copy.wait()

    @pl.loop(0, nk)
    def _(c):
        w_copy(c).wait()
        multiply(t, c)

    finish(t)
    combine(t)

    @pl.loop(1, nt)
    def _(step):
        left, right = t - step, t + step
        has_left, has_right = left >= 0, right < nt

        @pl.loop(0, nk)
        def _(c):
            @pl.when(has_left)
            def _():
                flow(0, left, c, False).wait_recv()

                @pl.when(t + 1 < nt)
                def _():
                    flow(0, left, c, False).start()

            @pl.when(has_right)
            def _():
                flow(1, right, c, False).wait_recv()

                @pl.when(t > 0)
                def _():
                    flow(1, right, c, False).start()

            @pl.when(has_left)
            def _():
                multiply(left, c)

            @pl.when(has_right)
            def _():
                multiply(right, c)

        @pl.when(has_left)
        def _():
            finish(left)

        @pl.when(has_right)
        def _():
            finish(right)

        @pl.when(has_left)
        def _():
            combine(left)

        @pl.when(has_right)
        def _():
            combine(right)

    @pl.loop(0, per_owner)
    def _(place):
        @pl.loop(0, nq)
        def _(other):
            @pl.when(other != q)
            def _():
                pltpu.make_async_remote_copy(
                    src_ref=rsend.at[0], dst_ref=rankbuf.at[place, other],
                    send_sem=rank_send.at[0], recv_sem=rank_recv.at[place, other],
                    device_id={"rep": 1 - r}, device_id_type=MESH).wait_recv()

        total = rankbuf[place, 0]
        for other in range(1, nq):
            total = total + rankbuf[place, other]
        lrbuf[place, :, lane_cols(t)] = total.astype(jnp.bfloat16)

        @pl.loop(0, nt)
        def _(other):
            @pl.when(other != t)
            def _():
                lr_copy(place, other, t).start()

    up_own.wait()

    @pl.loop(0, nq)
    def _(other):
        @pl.when(other != q)
        def _():
            up_copy(other, other).wait_recv()

    @pl.loop(0, per_owner)
    def _(place):
        @pl.loop(0, nq)
        def _(other):
            @pl.when(other != q)
            def _():
                pltpu.make_async_remote_copy(
                    src_ref=halfbuf.at[0], dst_ref=basebuf.at[place, other // nr, other % nr],
                    send_sem=base_send.at[0], recv_sem=base_recv.at[place, other],
                    device_id={"rep": 1 - r}, device_id_type=MESH).wait_recv()

        @pl.loop(0, nt)
        def _(other):
            @pl.when(other != t)
            def _():
                lr_copy(place, other, other).wait_recv()

        spread = lrbuf[place]
        out_rows = pl.ds(pl.multiple_of(place * rows, rows), rows)
        for part in range(nr):
            total = basebuf[place, 0, part]
            for other in range(1, ng):
                total = total + basebuf[place, other, part]
            at = slice(part * half, (part + 1) * half)
            delta = jnp.dot(spread, upbuf[:, at], preferred_element_type=jnp.float32)
            out_ref[out_rows, at] = (total + adapter_scale * delta).astype(jnp.bfloat16)

    @pl.loop(0, nk)
    def _(c):
        @pl.when(t + 1 < nt)
        def _():
            flow(0, t, c, True).wait_send()

            @pl.loop(0, t)
            def _(block):
                flow(0, block, c, False).wait_send()

        @pl.when(t > 0)
        def _():
            flow(1, t, c, True).wait_send()

            @pl.loop(t + 1, nt)
            def _(block):
                flow(1, block, c, False).wait_send()

    @pl.loop(0, nq)
    def _(other):
        @pl.when(other != q)
        def _():
            up_copy(other, q).wait_send()

    @pl.loop(0, nt)
    def _(block):
        owner, place = block // per_owner, block % per_owner
        half_copy(block).wait_send()

        @pl.when(owner != q)
        def _():
            base_copy(block, owner, place).wait_send()
            rank_copy(block, owner, place).wait_send()

    @pl.loop(0, per_owner)
    def _(place):
        @pl.loop(0, nt)
        def _(other):
            @pl.when(other != t)
            def _():
                lr_copy(place, other, t).wait_send()


def on_device(hidden_rows, down_weight, adapter_down, adapter_up, adapter_id, adapter_slot):
    nt, ng, nr = (lax.axis_size(name) for name in ("tensor", "group", "rep"))
    nq = ng * nr
    rows, depth = hidden_rows.shape
    width = down_weight.shape[1]
    slots, _, rank = adapter_down.shape
    up_rows = adapter_up.shape[0] * rank
    lanes = slots * rank
    per_owner = nt // nq
    nk = next(n for n in (7, 2, 1) if depth % (n * 128) == 0 and nt * n <= 64)
    tile = min(512, width)
    up_flat = adapter_up.reshape(up_rows, width)
    anywhere = pl.BlockSpec(memory_space=pl.ANY)
    f32, bf16 = jnp.float32, jnp.bfloat16
    dma = pltpu.SemaphoreType.DMA
    return pl.pallas_call(
        functools.partial(kernel, nt, ng, nr, nk, tile),
        out_shape=jax.ShapeDtypeStruct((per_owner * rows, width), bf16),
        in_specs=[anywhere] * 4 + [
            pl.BlockSpec(memory_space=pltpu.VMEM), pl.BlockSpec(memory_space=pltpu.SMEM)],
        out_specs=pl.BlockSpec(memory_space=pltpu.VMEM),
        scratch_shapes=[
            pltpu.VMEM((depth, width), bf16),
            pltpu.VMEM((slots, depth, rank), bf16),
            pltpu.VMEM((nt, rows, depth), bf16),
            pltpu.VMEM((nq * up_rows, width), bf16),
            pltpu.VMEM((nt, rows, width), f32),
            pltpu.VMEM((nt, rows, lanes), f32),
            pltpu.VMEM((nt, rows, lanes), f32),
            pltpu.VMEM((nt, rows, width // nr), f32),
            pltpu.VMEM((per_owner, ng, nr, rows, width // nr), f32),
            pltpu.VMEM((per_owner, nq, rows, lanes), f32),
            pltpu.VMEM((per_owner, rows, nt * lanes), bf16),
            dma((nk,)), dma, dma, dma,
            dma((2, nt, nk)), dma((nt, nk)), dma((nq,)), dma((nq,)),
            dma((nt,)), dma((nt,)), dma((nt,)), dma((per_owner, nq)),
            dma((nt,)), dma((per_owner, nq)), dma((per_owner, nt)), dma((per_owner, nt)),
        ],
        compiler_params=pltpu.CompilerParams(
            collective_id=0, has_side_effects=True, vmem_limit_bytes=58 * 2**20),
    )(hidden_rows, down_weight, adapter_down, up_flat, adapter_id, adapter_slot)


def solution(mesh):
    placed = (
        P(("parts", "tensor"), ("group", "rep")),
        P(("group", "rep"), "tensor"),
        P("tensor", ("group", "rep"), None),
        P(("group", "rep"), None, "tensor"),
        P("parts", None),
        P(),
    )
    return jax.shard_map(
        on_device,
        mesh=mesh,
        in_specs=placed,
        out_specs=P(("parts", "group", "rep"), "tensor"),
        check_vma=False,
    )
```

time: 160 us -> 85.5 us (0.53)
  Pallas kernels: 0 us -> 77.6 us
  waiting for transfers between devices: 77.2 us -> 0 us
  blocking collectives: 26.9 us -> 0 us
  matrix products: 22.5 us -> 0 us
  between operations: 13.3 us -> 0.01 us
  local copies, waits for them, and re-layouts: 16.5 us -> 7.71 us
  other arithmetic: 3.85 us -> 0 us
    pallas_call x0 -> x1, Pallas kernels: none -> 77.6 us  [on_device(): pl.pallas_call(functools.partial(kernel, nt, ng, nr, nk, tile), out_shape...]
    all_gather x2 -> x0, waiting for transfers between devices: 75.7 us -> none  [the longest x1 75.7 us: on_device(): gathered = lax.all_gather(hidden_rows, 'tensor', axis=0, tiled=True)]
    dot_general x3 -> x0, matrix products: 22.5 us -> none  [the longest x1 16 us: on_device(): jnp.dot(gathered, down_weight, preferred_element_type=jnp.float32)]
    gather x5 -> x0, local copies, waits for them, and re-layouts: 14.6 us -> none  [the longest x1 10.5 us: on_device(): gathered[rows_index]]
    psum x1 -> x0, blocking collectives: 13.5 us -> none  [on_device(): summed = lax.psum(partial_rank, ('group', 'rep'))]
    all_gather x1 -> x0, blocking collectives: 13.4 us -> none  [on_device(): lax.all_gather(summed.astype(jnp.bfloat16), 'tensor', axis=0, tiled=True)]
    unnamed x6 -> x3, local copies, waits for them, and re-layouts: 0.01 us -> 7.71 us
    sort x1 -> x0, other arithmetic: 3.17 us -> none  [on_device(): sort_order = jnp.argsort(slot_of_row, stable=True)]
  transfers between devices with their start and end apart: 3 -> 0, of which waited for: 1 -> 0; matrix products, arithmetic and copies ran while one was open for 25% -> 0% of each run, Pallas kernels for 0% -> 0%
where the time goes in v1:
time: 85.5 us; the launch traced here: 85.3 us
  Pallas kernels  77.6 us (91%)
  local copies, waits for them, and re-layouts  7.71 us (9%)
    pallas_call x1, Pallas kernels, on_device(): pl.pallas_call(functools.partial(kernel, nt, ng, nr, nk, tile), out_shape...  77.6 us
    unnamed x3, local copies, waits for them, and re-layouts  7.71 us

profile of v1, /device:TPU:0, one launch (start us, length us, event | category | flops | bytes accessed | tf_op | source)
XLA Modules:
  0.0 85.3 jit_solution(15595881157440691993)
XLA Ops:
  0.0 1.5 %copy.8.id_ref = s32[256,1]{1,0:T(8,128)} copy(s32[256,1]{0,1:T(1,128)} %param.10) | data formatting | bytes 2048 | tf_op args[4]
  1.5 4.6 %copy.7.a_ref = bf16[2,7168,64]{2,1,0:T(8,128)(2,1)} copy(bf16[2,7168,64]{1,2,0:T(8,128)(2,1)} %param.8) | data formatting | bytes 3670016 | tf_op args[2]
  6.0 77.6 %shard_map.64 = bf16[64,2048]{1,0:T(8,128)(2,1)} custom-call(bf16[64,7168]{1,0:T(8,128)(2,1)} %h_ref.1, bf16[7168,2048]{1,0:T(8,128)(2,1)} %w_ref.1, bf16[2,7168,64]{2,1,0:T(8,128)(2,1)} %copy.7.a_ref, bf16[128,2048]{1,0:T(8,128)(2,1)} %bitcast.1, s32[256,1]{1,0:T(8,128)} %copy.8.id_ref, s32[8]{0:T(128)} %slot_ref.1), custom_call_target="tpu_custom_call" | custom-call | tf_op jit(solution)/shard_map/pallas_call | solution.py:359
  83.6 1.7 %copy.10 = bf16[64,2048]{1,0:T(8,128)(2,1)} copy(bf16[64,2048]{1,0:T(8,128)(2,1)} %shard_map.64) | data formatting | bytes 524288

commit v2 on v1

--- a/solution.py
+++ b/solution.py
@@ -11,9 +11,9 @@
 
 
 def kernel(
-    nt, ng, nr, nk, tile,
+    nt, ng, nr, nk, tile, rank,
     h_ref, w_ref, a_ref, up_ref, id_ref, slot_ref, out_ref,
-    wv, av, hbuf, upbuf, acc, racc, rsend, halfbuf, basebuf, rankbuf, lrbuf,
+    wv, av, hbuf, upbuf, acc, racc, chosen, rsend, halfbuf, basebuf, rankbuf, lrbuf,
     w_sem, a_sem, own_sem, up_own_sem, flow_send, flow_recv, up_send, up_recv,
     half_send, half_recv, base_send, base_recv, rank_send, rank_recv, lr_send, lr_recv,
 ):
@@ -25,8 +25,8 @@
     width = w_ref.shape[1]
     half = width // nr
     kc = depth // nk
-    slots, _, rank = av.shape
-    lanes = slots * rank
+    lanes = av.shape[0]
+    slots = lanes // rank
     up_rows = up_ref.shape[0]
     adapters = slot_ref.shape[0]
 
@@ -134,6 +134,14 @@
 
     acc[...] = jnp.zeros_like(acc)
     racc[...] = jnp.zeros_like(racc)
+    ids = id_ref[...]
+    row_slot = jnp.zeros_like(ids)
+    for adapter in range(adapters):
+        row_slot = row_slot + jnp.where(ids == adapter, slot_ref[adapter], 0)
+    lane = lax.broadcasted_iota(jnp.int32, (lanes, nt * rows), 0)
+    first = jnp.broadcast_to((row_slot - t * slots) * rank, (lanes, nt * rows))
+    named = jnp.where((lane >= first) & (lane < first + rank), 1.0, 0.0).astype(jnp.float32)
+    chosen[...] = jnp.transpose(named).reshape(nt, rows, lanes)
 
     def multiply(block, c):
         x = hbuf[block, :, cols(c)]
@@ -144,19 +152,12 @@
             acc[block, :, at] += jnp.dot(
                 x, wv[cols(c), at], preferred_element_type=jnp.float32)
 
-        racc[block] += jnp.concatenate(
-            [jnp.dot(x, av[s, cols(c), :], preferred_element_type=jnp.float32)
-             for s in range(slots)], axis=1)
+        racc[block] += lax.dot_general(
+            x, av[:, cols(c)], (((1,), (1,)), ((), ())), preferred_element_type=jnp.float32)
 
     def finish(block):
         owner, place = block // per_owner, block % per_owner
-        ids = id_ref[pl.ds(pl.multiple_of(block * rows, rows), rows), :]
-        row_slot = jnp.zeros_like(ids)
-        for adapter in range(adapters):
-            row_slot = row_slot + jnp.where(ids == adapter, slot_ref[adapter], 0)
-        lane = lax.broadcasted_iota(jnp.int32, (rows, lanes), 1)
-        first = (row_slot - t * slots) * rank
-        masked = jnp.where((lane >= first) & (lane < first + rank), racc[block], 0.0)
+        masked = jnp.where(chosen[block] > 0.5, racc[block], 0.0)
 
         @pl.when(owner == q)
         def _():
@@ -352,22 +353,24 @@
     per_owner = nt // nq
     nk = next(n for n in (7, 2, 1) if depth % (n * 128) == 0 and nt * n <= 64)
     tile = min(512, width)
+    down_flat = jnp.swapaxes(adapter_down, 1, 2).reshape(lanes, depth)
     up_flat = adapter_up.reshape(up_rows, width)
     anywhere = pl.BlockSpec(memory_space=pl.ANY)
     f32, bf16 = jnp.float32, jnp.bfloat16
     dma = pltpu.SemaphoreType.DMA
     return pl.pallas_call(
-        functools.partial(kernel, nt, ng, nr, nk, tile),
+        functools.partial(kernel, nt, ng, nr, nk, tile, rank),
         out_shape=jax.ShapeDtypeStruct((per_owner * rows, width), bf16),
         in_specs=[anywhere] * 4 + [
             pl.BlockSpec(memory_space=pltpu.VMEM), pl.BlockSpec(memory_space=pltpu.SMEM)],
         out_specs=pl.BlockSpec(memory_space=pltpu.VMEM),
         scratch_shapes=[
             pltpu.VMEM((depth, width), bf16),
-            pltpu.VMEM((slots, depth, rank), bf16),
+            pltpu.VMEM((lanes, depth), bf16),
             pltpu.VMEM((nt, rows, depth), bf16),
             pltpu.VMEM((nq * up_rows, width), bf16),
             pltpu.VMEM((nt, rows, width), f32),
+            pltpu.VMEM((nt, rows, lanes), f32),
             pltpu.VMEM((nt, rows, lanes), f32),
             pltpu.VMEM((nt, rows, lanes), f32),
             pltpu.VMEM((nt, rows, width // nr), f32),
@@ -381,7 +384,7 @@
         ],
         compiler_params=pltpu.CompilerParams(
             collective_id=0, has_side_effects=True, vmem_limit_bytes=58 * 2**20),
-    )(hidden_rows, down_weight, adapter_down, up_flat, adapter_id, adapter_slot)
+    )(hidden_rows, down_weight, down_flat, up_flat, adapter_id.reshape(1, -1), adapter_slot)
 
 
 def solution(mesh):

time: 85.5 us -> 79.1 us (0.925)
  local copies, waits for them, and re-layouts: 7.71 us -> 1.67 us
    unnamed x3 -> x1, local copies, waits for them, and re-layouts: 7.71 us -> 1.67 us
where the time goes in v2:
time: 79.1 us; the launch traced here: 78.9 us
  Pallas kernels  77.2 us (98%)
  local copies, waits for them, and re-layouts  1.67 us (2%)
    pallas_call x1, Pallas kernels, on_device(): pl.pallas_call(functools.partial(kernel, nt, ng, nr, nk, tile, rank), out...  77.2 us
    unnamed x1, local copies, waits for them, and re-layouts  1.67 us

profile of v2, /device:TPU:0, one launch (start us, length us, event | category | flops | bytes accessed | tf_op | source)
XLA Modules:
  0.0 78.9 jit_solution(4907412943333608620)
XLA Ops:
  0.0 77.2 %shard_map.64 = bf16[64,2048]{1,0:T(8,128)(2,1)} custom-call(bf16[64,7168]{1,0:T(8,128)(2,1)} %h_ref.1, bf16[7168,2048]{1,0:T(8,128)(2,1)} %w_ref.1, bf16[128,7168]{1,0:T(8,128)(2,1)} %bitcast.5, bf16[128,2048]{1,0:T(8,128)(2,1)} %bitcast.6, s32[1,256]{1,0:T(1,128)} %bitcast.7, s32[8]{0:T(128)} %slot_ref.1), custom_call_target="tpu_custom_call" | custom-call | tf_op jit(solution)/shard_map/pallas_call | solution.py:361
  77.3 1.7 %copy.8 = bf16[64,2048]{1,0:T(8,128)(2,1)} copy(bf16[64,2048]{1,0:T(8,128)(2,1)} %shard_map.64) | data formatting | bytes 524288

commit v3 on v2

--- a/solution.py
+++ b/solution.py
@@ -39,11 +39,10 @@
     def lane_cols(index):
         return pl.ds(pl.multiple_of(index * lanes, 128), lanes)
 
-    def flow(direction, block, c, own):
-        source = h_ref.at[:, cols(c)] if own else hbuf.at[block, :, cols(c)]
+    def flow(direction, block, c):
         target = t + 1 if direction == 0 else t - 1
         return pltpu.make_async_remote_copy(
-            src_ref=source, dst_ref=hbuf.at[block, :, cols(c)],
+            src_ref=hbuf.at[block, c], dst_ref=hbuf.at[block, c],
             send_sem=flow_send.at[direction, block, c], recv_sem=flow_recv.at[block, c],
             device_id={"tensor": target}, device_id_type=MESH)
 
@@ -85,11 +84,16 @@
             send_sem=lr_send.at[place, target], recv_sem=lr_recv.at[place, source],
             device_id={"tensor": target}, device_id_type=MESH)
 
-    own_copy = pltpu.make_async_copy(h_ref, hbuf.at[t], own_sem)
+    def own_copy(c):
+        return pltpu.make_async_copy(h_ref.at[:, cols(c)], hbuf.at[t, c], own_sem.at[c])
+
     a_copy = pltpu.make_async_copy(a_ref, av, a_sem)
     up_own = pltpu.make_async_copy(up_ref, upbuf.at[up_rows_of(q)], up_own_sem)
 
-    own_copy.start()
+    @pl.loop(0, nk)
+    def _(c):
+        own_copy(c).start()
+
     a_copy.start()
 
     @pl.loop(0, nk)
@@ -118,13 +122,15 @@
 
     @pl.loop(0, nk)
     def _(c):
+        own_copy(c).wait()
+
         @pl.when(t + 1 < nt)
         def _():
-            flow(0, t, c, True).start()
+            flow(0, t, c).start()
 
         @pl.when(t > 0)
         def _():
-            flow(1, t, c, True).start()
+            flow(1, t, c).start()
 
     @pl.loop(0, nq)
     def _(other):
@@ -144,7 +150,7 @@
     chosen[...] = jnp.transpose(named).reshape(nt, rows, lanes)
 
     def multiply(block, c):
-        x = hbuf[block, :, cols(c)]
+        x = hbuf[block, c]
 
         @pl.loop(0, width // tile)
         def _(n):
@@ -184,7 +190,6 @@
             acc[block, :, half_cols(r)] = value
             base_copy(block, owner, place).start()
 
-    own_copy.wait()
     a_copy.wait()
 
     @pl.loop(0, nk)
@@ -204,19 +209,19 @@
         def _(c):
             @pl.when(has_left)
             def _():
-                flow(0, left, c, False).wait_recv()
+                flow(0, left, c).wait_recv()
 
                 @pl.when(t + 1 < nt)
                 def _():
-                    flow(0, left, c, False).start()
+                    flow(0, left, c).start()
 
             @pl.when(has_right)
             def _():
-                flow(1, right, c, False).wait_recv()
+                flow(1, right, c).wait_recv()
 
                 @pl.when(t > 0)
                 def _():
-                    flow(1, right, c, False).start()
+                    flow(1, right, c).start()
 
             @pl.when(has_left)
             def _():
@@ -297,25 +302,25 @@
                 total = total + basebuf[place, other, part]
             at = slice(part * half, (part + 1) * half)
             delta = jnp.dot(spread, upbuf[:, at], preferred_element_type=jnp.float32)
-            out_ref[out_rows, at] = (total + adapter_scale * delta).astype(jnp.bfloat16)
+            out_ref[out_rows, at] = total + adapter_scale * delta
 
     @pl.loop(0, nk)
     def _(c):
         @pl.when(t + 1 < nt)
         def _():
-            flow(0, t, c, True).wait_send()
+            flow(0, t, c).wait_send()
 
             @pl.loop(0, t)
             def _(block):
-                flow(0, block, c, False).wait_send()
+                flow(0, block, c).wait_send()
 
         @pl.when(t > 0)
         def _():
-            flow(1, t, c, True).wait_send()
+            flow(1, t, c).wait_send()
 
             @pl.loop(t + 1, nt)
             def _(block):
-                flow(1, block, c, False).wait_send()
+                flow(1, block, c).wait_send()
 
     @pl.loop(0, nq)
     def _(other):
@@ -360,14 +365,14 @@
     dma = pltpu.SemaphoreType.DMA
     return pl.pallas_call(
         functools.partial(kernel, nt, ng, nr, nk, tile, rank),
-        out_shape=jax.ShapeDtypeStruct((per_owner * rows, width), bf16),
+        out_shape=jax.ShapeDtypeStruct((per_owner * rows, width), f32),
         in_specs=[anywhere] * 4 + [
             pl.BlockSpec(memory_space=pltpu.VMEM), pl.BlockSpec(memory_space=pltpu.SMEM)],
         out_specs=pl.BlockSpec(memory_space=pltpu.VMEM),
         scratch_shapes=[
             pltpu.VMEM((depth, width), bf16),
             pltpu.VMEM((lanes, depth), bf16),
-            pltpu.VMEM((nt, rows, depth), bf16),
+            pltpu.VMEM((nt, nk, rows, depth // nk), bf16),
             pltpu.VMEM((nq * up_rows, width), bf16),
             pltpu.VMEM((nt, rows, width), f32),
             pltpu.VMEM((nt, rows, lanes), f32),
@@ -377,14 +382,14 @@
             pltpu.VMEM((per_owner, ng, nr, rows, width // nr), f32),
             pltpu.VMEM((per_owner, nq, rows, lanes), f32),
             pltpu.VMEM((per_owner, rows, nt * lanes), bf16),
-            dma((nk,)), dma, dma, dma,
+            dma((nk,)), dma, dma((nk,)), dma,
             dma((2, nt, nk)), dma((nt, nk)), dma((nq,)), dma((nq,)),
             dma((nt,)), dma((nt,)), dma((nt,)), dma((per_owner, nq)),
             dma((nt,)), dma((per_owner, nq)), dma((per_owner, nt)), dma((per_owner, nt)),
         ],
         compiler_params=pltpu.CompilerParams(
             collective_id=0, has_side_effects=True, vmem_limit_bytes=58 * 2**20),
-    )(hidden_rows, down_weight, down_flat, up_flat, adapter_id.reshape(1, -1), adapter_slot)
+    )(hidden_rows, down_weight, down_flat, up_flat, adapter_id.reshape(1, -1), adapter_slot).astype(bf16)
 
 
 def solution(mesh):

time: 79.1 us -> 79.2 us (level)
  other arithmetic: 0 us -> 1.77 us
  local copies, waits for them, and re-layouts: 1.67 us -> 0 us
    convert_element_type x0 -> x1, other arithmetic: none -> 1.77 us  [on_device(): return pl.pallas_call(functools.partial(kernel, nt, ng, nr, nk, tile, ran...]
    unnamed x1 -> x0, local copies, waits for them, and re-layouts: 1.67 us -> none
where the time goes in v3:
time: 79.2 us; the launch traced here: 79.1 us
  Pallas kernels  77.3 us (98%)
  other arithmetic  1.77 us (2%)
    pallas_call x1, Pallas kernels, on_device(): pl.pallas_call(functools.partial(kernel, nt, ng, nr, nk, tile, rank), out...  77.3 us
    convert_element_type x1, other arithmetic, on_device(): return pl.pallas_call(functools.partial(kernel, nt, ng, nr, nk, tile, ran...  1.77 us

profile of v3, /device:TPU:0, one launch (start us, length us, event | category | flops | bytes accessed | tf_op | source)
XLA Modules:
  0.0 79.1 jit_solution(10021692755346981355)
XLA Ops:
  0.0 77.3 %shard_map.64 = f32[64,2048]{1,0:T(8,128)} custom-call(bf16[64,7168]{1,0:T(8,128)(2,1)} %h_ref.1, bf16[7168,2048]{1,0:T(8,128)(2,1)} %w_ref.1, bf16[128,7168]{1,0:T(8,128)(2,1)} %bitcast.5, bf16[128,2048]{1,0:T(8,128)(2,1)} %bitcast.6, s32[1,256]{1,0:T(1,128)} %bitcast.7, s32[8]{0:T(128)} %slot_ref.1), custom_call_target="tpu_custom_call" | custom-call | tf_op jit(solution)/shard_map/pallas_call | solution.py:366
  77.3 1.8 %convert_element_type.3 = bf16[64,2048]{1,0:T(8,128)(2,1)} convert(f32[64,2048]{1,0:T(8,128)} %shard_map.64) | non-fusion elementwise | flops 131072 | bytes 786432 | tf_op jit(solution)/shard_map/convert_element_type | solution.py:392
